TPU v7x, 256 devices: a whole 4x4x8 slice. The times are simulated.
256 devices in a mesh: dp: 32 (over y, x, core), ulysses: 8 (over z).
Axes of the slice: x: 4, y: 4, z: 8, core: 2. Of those that a mesh axis runs over, the one named last changes fastest.
Arguments:
- query_in: bfloat16 [65536, 3072], P(('dp', 'ulysses')), may hold values from -6 to 6
- key_in: bfloat16 [65536, 3072], P(('dp', 'ulysses')), may hold values from -6 to 6
- value_in: bfloat16 [65536, 3072], P(('dp', 'ulysses')), may hold values from -6 to 6
- grad_out: bfloat16 [65536, 3072], P('dp', 'ulysses'), may hold values from -6 to 6
- packing: int32 [512], replicated, may hold values from 0 to 511, as said below
- doc_tiles: int32 [32, 5], P('dp'), may hold values from 1 to 4, 16 in all within a row
Outputs:
- attended: bfloat16 [65536, 3072], P('dp', 'ulysses')
- grad_query: bfloat16 [65536, 3072], P(('dp', 'ulysses'))
- grad_key: bfloat16 [65536, 3072], P(('dp', 'ulysses'))
- grad_value: bfloat16 [65536, 3072], P(('dp', 'ulysses'))
Inputs may be any that keep to these rules, and one draw needn't show every extreme that they name: packing fills every packed tile exactly once; tile g goes to packed row packing[g] // 16, slot packing[g] % 16; from the 16 tiles of one delivered row at most 1 go to one packed row, and that many do for some pairs of rows in every draw. Each row of doc_tiles sums to 16, and in each row some document has 4 tiles.
All inputs are finite; a program needn't handle non-finite values.
Results may differ from a plain program's by a relative error of at most 0.028.
Values may be sent and summed in bfloat16 or wider, within the bound.
No kernel may reach another device: no remote copies, remote signals or barrier semaphores. Data moves between devices by JAX's collectives and lax.ppermute only.
A program may use at most 128 MiB of HBM per device.

v0:
```python
import jax
import jax.numpy as jnp
from jax import lax
from jax.sharding import PartitionSpec as P

HEAD_DIM = 128
TILE = 128
DOC_MOST = 4
ROW_TOK = 2048
TILES = 16


def move_tables(packing, row_index, dp_count):
    capacity = max(1, TILES // dp_count)
    dest_plan = packing.reshape(dp_count, TILES)
    dest_rank = dest_plan // TILES
    dest_slot = dest_plan % TILES
    tile_index = jnp.arange(TILES, dtype=jnp.int32)
    earlier = tile_index[None, :] < tile_index[:, None]
    same_dest = dest_rank[:, :, None] == dest_rank[:, None, :]
    send_order = jnp.sum((same_dest & earlier[None]).astype(jnp.int32), axis=2, dtype=jnp.int32)
    slot_index = jnp.arange(dp_count * capacity, dtype=jnp.int32)
    peer_index = slot_index // capacity
    peer_place = slot_index % capacity
    own_rank = lax.dynamic_index_in_dim(dest_rank, row_index, 0, keepdims=False)
    own_order = lax.dynamic_index_in_dim(send_order, row_index, 0, keepdims=False)
    send_table = (
        (own_rank[None, :] == peer_index[:, None]) & (own_order[None, :] == peer_place[:, None])
    ).astype(jnp.bfloat16)
    arrive = dest_rank == row_index
    slot_hit = ((dest_slot[:, :, None] == tile_index[None, None, :]) & arrive[:, :, None]).astype(
        jnp.float32
    )
    rank_hit = (
        send_order[:, :, None] == jnp.arange(capacity, dtype=jnp.int32)[None, None, :]
    ).astype(jnp.float32)
    recv_table = jnp.einsum("stp,stc->psc", slot_hit, rank_hit)
    recv_table = recv_table.reshape(TILES, dp_count * capacity).astype(jnp.bfloat16)
    return (send_table, recv_table)


def select_tiles(tile_table, source):
    flat_tiles = source.reshape(tile_table.shape[1], -1)
    return jnp.dot(tile_table, flat_tiles, preferred_element_type=jnp.float32).astype(jnp.bfloat16)


def attend_heads(query_rows, key_rows, value_rows, grad_rows, doc_of):
    heads = query_rows.shape[1]
    block_tiles = 4
    block_rows = block_tiles * TILE
    margin = (DOC_MOST - 1) * TILE
    reach = DOC_MOST * TILE
    blocks = ROW_TOK // block_rows
    score_scale = HEAD_DIM ** (-0.5)
    pad_rows = jnp.zeros((margin, heads, HEAD_DIM), jnp.bfloat16)
    key_padded = jnp.concatenate([pad_rows, key_rows], axis=0)
    value_padded = jnp.concatenate([pad_rows, value_rows], axis=0)
    doc_padded = jnp.concatenate([jnp.full((margin,), -1, jnp.int32), doc_of])
    reach_pos = jnp.arange(reach, dtype=jnp.int32)
    tile_offsets = jnp.arange(block_tiles, dtype=jnp.int32) * TILE

    def windows(source, start):
        return jnp.stack(
            [
                lax.dynamic_slice_in_dim(source, start + offset * TILE, reach, 0)
                for offset in range(block_tiles)
            ]
        )

    def one_block(carry, block_index):
        grad_key_sum, grad_value_sum = carry
        start = block_index * block_rows
        query_block = lax.dynamic_slice_in_dim(query_rows, start, block_rows, 0).reshape(
            block_tiles, TILE, heads, HEAD_DIM
        )
        grad_block = lax.dynamic_slice_in_dim(grad_rows, start, block_rows, 0).reshape(
            block_tiles, TILE, heads, HEAD_DIM
        )
        query_docs = lax.dynamic_slice_in_dim(doc_of, start, block_rows, 0).reshape(
            block_tiles, TILE
        )
        key_tiles = windows(key_padded, start)
        value_tiles = windows(value_padded, start)
        key_docs = windows(doc_padded, start)
        query_pos = start + jnp.arange(block_rows, dtype=jnp.int32).reshape(block_tiles, TILE)
        key_pos = start - margin + tile_offsets[:, None] + reach_pos[None, :]
        allowed = (query_docs[:, :, None] == key_docs[:, None, :]) & (
            query_pos[:, :, None] >= key_pos[:, None, :]
        )
        scores = (
            jnp.einsum(
                "tqhd,tkhd->htqk", query_block, key_tiles, preferred_element_type=jnp.float32
            )
            * score_scale
        )
        scores = jnp.where(allowed[None], scores, -jnp.inf)
        row_top = jnp.max(scores, axis=3, keepdims=True)
        weights = jnp.exp(scores - row_top)
        softmax_probs = weights / jnp.sum(weights, axis=3, keepdims=True)
        probs_low = softmax_probs.astype(jnp.bfloat16)
        attended = jnp.einsum(
            "htqk,tkhd->tqhd", probs_low, value_tiles, preferred_element_type=jnp.float32
        ).astype(jnp.bfloat16)
        row_delta = jnp.sum(grad_block.astype(jnp.float32) * attended.astype(jnp.float32), axis=3)
        grad_value_part = jnp.einsum(
            "htqk,tqhd->tkhd", probs_low, grad_block, preferred_element_type=jnp.float32
        )
        grad_probs = jnp.einsum(
            "tqhd,tkhd->htqk", grad_block, value_tiles, preferred_element_type=jnp.float32
        )
        grad_scores = (
            softmax_probs * (grad_probs - row_delta.transpose(2, 0, 1)[:, :, :, None]) * score_scale
        ).astype(jnp.bfloat16)
        grad_query = jnp.einsum(
            "htqk,tkhd->tqhd", grad_scores, key_tiles, preferred_element_type=jnp.float32
        ).astype(jnp.bfloat16)
        grad_key_part = jnp.einsum(
            "htqk,tqhd->tkhd", grad_scores, query_block, preferred_element_type=jnp.float32
        )
        for offset in range(block_tiles):
            place = start + offset * TILE
            key_slice = (
                lax.dynamic_slice_in_dim(grad_key_sum, place, reach, 0) + grad_key_part[offset]
            )
            value_slice = (
                lax.dynamic_slice_in_dim(grad_value_sum, place, reach, 0) + grad_value_part[offset]
            )
            grad_key_sum = lax.dynamic_update_slice_in_dim(grad_key_sum, key_slice, place, 0)
            grad_value_sum = lax.dynamic_update_slice_in_dim(grad_value_sum, value_slice, place, 0)
        return (
            (grad_key_sum, grad_value_sum),
            (
                attended.reshape(block_rows, heads, HEAD_DIM),
                grad_query.reshape(block_rows, heads, HEAD_DIM),
            ),
        )

    zero_sums = jnp.zeros((margin + ROW_TOK, heads, HEAD_DIM), jnp.float32)
    final_sums, block_outs = lax.scan(
        one_block, (zero_sums, zero_sums), jnp.arange(blocks, dtype=jnp.int32)
    )
    attended = block_outs[0].reshape(ROW_TOK, heads * HEAD_DIM)
    grad_query = block_outs[1].reshape(ROW_TOK, heads * HEAD_DIM)
    grad_key = final_sums[0][margin:].astype(jnp.bfloat16).reshape(ROW_TOK, heads * HEAD_DIM)
    grad_value = final_sums[1][margin:].astype(jnp.bfloat16).reshape(ROW_TOK, heads * HEAD_DIM)
    return (attended, grad_query, grad_key, grad_value)


def shards(query_in, key_in, value_in, grad_out, packing, doc_tiles):
    dp_count = lax.axis_size("dp")
    row_index = lax.axis_index("dp")
    send_table, recv_table = move_tables(packing, row_index, dp_count)
    query_row, key_row, value_row = (
        lax.all_to_all(query_in, "ulysses", split_axis=1, concat_axis=0, tiled=True),
        lax.all_to_all(key_in, "ulysses", split_axis=1, concat_axis=0, tiled=True),
        lax.all_to_all(value_in, "ulysses", split_axis=1, concat_axis=0, tiled=True),
    )
    row_width = query_row.shape[1]
    heads = row_width // HEAD_DIM
    query_got, key_got, value_got = (
        lax.all_to_all(
            select_tiles(send_table, query_row), "dp", split_axis=0, concat_axis=0, tiled=True
        ),
        lax.all_to_all(
            select_tiles(send_table, key_row), "dp", split_axis=0, concat_axis=0, tiled=True
        ),
        lax.all_to_all(
            select_tiles(send_table, value_row), "dp", split_axis=0, concat_axis=0, tiled=True
        ),
    )
    query_packed = select_tiles(recv_table, query_got).reshape(ROW_TOK, heads, HEAD_DIM)
    key_packed = select_tiles(recv_table, key_got).reshape(ROW_TOK, heads, HEAD_DIM)
    value_packed = select_tiles(recv_table, value_got).reshape(ROW_TOK, heads, HEAD_DIM)
    grad_rows = grad_out.reshape(ROW_TOK, heads, HEAD_DIM)
    bounds = jnp.cumsum(doc_tiles[0], dtype=jnp.int32)
    tile_index = jnp.arange(TILES, dtype=jnp.int32)
    tile_docs = jnp.sum(
        (bounds[None, :] <= tile_index[:, None]).astype(jnp.int32), axis=1, dtype=jnp.int32
    )
    doc_of = jnp.repeat(tile_docs, TILE)
    return_table = recv_table.T
    anchor_table = send_table.T
    attended, grad_query, grad_key, grad_value = attend_heads(
        query_packed, key_packed, value_packed, grad_rows, doc_of
    )
    query_home, key_home, value_home = (
        lax.all_to_all(
            select_tiles(return_table, grad_query), "dp", split_axis=0, concat_axis=0, tiled=True
        ),
        lax.all_to_all(
            select_tiles(return_table, grad_key), "dp", split_axis=0, concat_axis=0, tiled=True
        ),
        lax.all_to_all(
            select_tiles(return_table, grad_value), "dp", split_axis=0, concat_axis=0, tiled=True
        ),
    )
    query_anchor = select_tiles(anchor_table, query_home).reshape(ROW_TOK, row_width)
    key_anchor = select_tiles(anchor_table, key_home).reshape(ROW_TOK, row_width)
    value_anchor = select_tiles(anchor_table, value_home).reshape(ROW_TOK, row_width)
    grad_query_out, grad_key_out, grad_value_out = (
        lax.all_to_all(query_anchor, "ulysses", split_axis=0, concat_axis=1, tiled=True),
        lax.all_to_all(key_anchor, "ulysses", split_axis=0, concat_axis=1, tiled=True),
        lax.all_to_all(value_anchor, "ulysses", split_axis=0, concat_axis=1, tiled=True),
    )
    return (attended, grad_query_out, grad_key_out, grad_value_out)


def solution(mesh):
    in_specs = (
        P(("dp", "ulysses"), None),
        P(("dp", "ulysses"), None),
        P(("dp", "ulysses"), None),
        P("dp", "ulysses"),
        P(),
        P("dp", None),
    )
    out_specs = (
        P("dp", "ulysses"),
        P(("dp", "ulysses"), None),
        P(("dp", "ulysses"), None),
        P(("dp", "ulysses"), None),
    )
    return jax.shard_map(shards, mesh=mesh, in_specs=in_specs, out_specs=out_specs, check_vma=False)
```

profile of v0, /device:TPU:6, one launch (start us, length us, event | category | flops | bytes accessed | tf_op | source)
XLA Modules:
  0.0 728.2 jit_solution(11247794292915253312)
XLA Ops:
  3.5 8.5 %all-to-all-start = ((bf16[256,8,384]{2,0,1:T(8,128)(2,1)}), bf16[256,8,384]{2,0,1:T(8,128)(2,1)S(1)}, u32[]{:S(2)}, u32[]{:S(2)}) async-start(bf16[256,8,384]{2,0,1:T(8,128)(2,1)} %bitcast.182), calls=%async_computation | async-start | bytes 3145728 | tf_op jit(solution)/shard_map/all_to_all | solution.py:154
  13.3 38.6 %all-to-all-done = bf16[256,8,384]{2,0,1:T(8,128)(2,1)S(1)} async-done(((bf16[256,8,384]{2,0,1:T(8,128)(2,1)}), bf16[256,8,384]{2,0,1:T(8,128)(2,1)S(1)}, u32[]{:S(2)}, u32[]{:S(2)}) %all-to-all-start) | async-done | bytes 1572896 | tf_op jit(solution)/shard_map/all_to_all | solution.py:154
  51.9 3.6 all-to-all-start.2
  58.2 35.4 %all-to-all-done.2 = bf16[256,8,384]{2,0,1:T(8,128)(2,1)S(1)} async-done(((bf16[256,8,384]{2,0,1:T(8,128)(2,1)}), bf16[256,8,384]{2,0,1:T(8,128)(2,1)S(1)}, u32[]{:S(2)}, u32[]{:S(2)}) %all-to-all-start.2) | async-done | bytes 1572896 | tf_op jit(solution)/shard_map/all_to_all | solution.py:155
  93.7 4.3 all-to-all-start.4
  103.2 3.8 reduce.5
  107.0 5.4 reshape.314
  112.4 26.0 %all-to-all-done.4 = bf16[256,8,384]{2,0,1:T(8,128)(2,1)} async-done(((bf16[256,8,384]{2,0,1:T(8,128)(2,1)}), bf16[256,8,384]{2,0,1:T(8,128)(2,1)}, u32[]{:S(2)}, u32[]{:S(2)}) %all-to-all-start.4) | async-done | bytes 1572896 | tf_op jit(solution)/shard_map/all_to_all | solution.py:156
  138.4 7.6 %all-to-all-start.3 = ((bf16[32,2,24576]{2,1,0:T(2,128)(2,1)}), bf16[32,2,24576]{2,1,0:T(2,128)(2,1)}, u32[]{:S(2)}, u32[]{:S(2)}) async-start(bf16[32,2,24576]{2,1,0:T(2,128)(2,1)} %reshape.314), calls=%async_computation.3 | async-start | bytes 6291456 | tf_op jit(solution)/shard_map/all_to_all | solution.py:164
  151.1 3.8 reduce.6
  154.9 5.4 reshape.316
  160.3 23.7 %all-to-all-done.3 = bf16[32,2,24576]{2,1,0:T(2,128)(2,1)} async-done(((bf16[32,2,24576]{2,1,0:T(2,128)(2,1)}), bf16[32,2,24576]{2,1,0:T(2,128)(2,1)}, u32[]{:S(2)}, u32[]{:S(2)}) %all-to-all-start.3) | async-done | bytes 3145760 | tf_op jit(solution)/shard_map/all_to_all | solution.py:164
  184.0 8.8 %all-to-all-start.5 = ((bf16[32,2,24576]{2,1,0:T(2,128)(2,1)}), bf16[32,2,24576]{2,1,0:T(2,128)(2,1)}, u32[]{:S(2)}, u32[]{:S(2)}) async-start(bf16[32,2,24576]{2,1,0:T(2,128)(2,1)} %reshape.316), calls=%async_computation.5 | async-start | bytes 6291456 | tf_op jit(solution)/shard_map/all_to_all | solution.py:167
  196.9 3.7 reduce.4
  200.6 5.4 reshape.312
  206.0 25.1 %all-to-all-done.5 = bf16[32,2,24576]{2,1,0:T(2,128)(2,1)} async-done(((bf16[32,2,24576]{2,1,0:T(2,128)(2,1)}), bf16[32,2,24576]{2,1,0:T(2,128)(2,1)}, u32[]{:S(2)}, u32[]{:S(2)}) %all-to-all-start.5) | async-done | bytes 3145760 | tf_op jit(solution)/shard_map/all_to_all | solution.py:167
  231.1 8.2 %all-to-all-start.1 = ((bf16[32,2,24576]{2,1,0:T(2,128)(2,1)}), bf16[32,2,24576]{2,1,0:T(2,128)(2,1)}, u32[]{:S(2)}, u32[]{:S(2)}) async-start(bf16[32,2,24576]{2,1,0:T(2,128)(2,1)} %reshape.312), calls=%async_computation.1 | async-start | bytes 6291456 | tf_op jit(solution)/shard_map/all_to_all | solution.py:161
  241.9 18.9 %reshape.317 = bf16[32,1,49152]{2,1,0:T(2,128)(2,1)} reshape(bf16[32,2,24576]{2,1,0:T(2,128)(2,1)} %all-to-all-done.5) | data formatting | bytes 6291456
  260.9 7.4 %convolution_convert_fusion.10 = bf16[16,49152]{1,0:T(8,128)(2,1)} fusion(bf16[32,1,49152]{2,1,0:T(2,128)(2,1)} %reshape.317, bf16[32,16]{1,0:T(8,128)(2,1)S(1)} %convert_element_type.107), kind=kOutput, calls=%fused_computation.89 | convolution fusion | flops 51118080 | bytes 4719616 | tf_op jit(solution)/shard_map/dot_general | solution.py:44
  273.0 18.9 %reshape.315 = bf16[32,1,49152]{2,1,0:T(2,128)(2,1)} reshape(bf16[32,2,24576]{2,1,0:T(2,128)(2,1)} %all-to-all-done.3) | data formatting | bytes 6291456
  291.9 7.4 %convolution_convert_fusion.11 = bf16[16,49152]{1,0:T(8,128)(2,1)} fusion(bf16[32,1,49152]{2,1,0:T(2,128)(2,1)} %reshape.315, bf16[32,16]{1,0:T(8,128)(2,1)S(1)} %convert_element_type.107), kind=kOutput, calls=%fused_computation.90 | convolution fusion | flops 51118080 | bytes 4719616 | tf_op jit(solution)/shard_map/dot_general | solution.py:44
  305.7 19.3 %reshape.313 = bf16[32,1,49152]{2,1,0:T(2,128)(2,1)} reshape(bf16[32,2,24576]{2,1,0:T(2,128)(2,1)} %all-to-all-done.1) | data formatting | bytes 6291456
  325.0 6.2 convolution_convert_fusion.12
  341.6 98.1 %while.19 = (s32[]{:T(128)}, f32[2432,3,128]{0,2,1:T(8,128)}, f32[2432,3,128]{0,2,1:T(8,128)}, bf16[4,512,3,128]{3,1,2,0:T(8,128)(2,1)}, bf16[4,512,3,128]{3,1,2...) while((s32[]{:T(128)}, f32[2432,3,128]{0,2,1:T(8,128)}, ...), condition=%wide.region_7.8_spmd.clone, body=%wide.region_3.7_spmd.clone.sunk | while | flops 1233527296 | bytes 161199440 | solution.py:139
  447.2 3.8 reduce.7
  451.0 5.5 reshape.318
  456.5 7.5 %all-to-all-start.6 = ((bf16[32,2,24576]{2,1,0:T(2,128)(2,1)}), bf16[32,2,24576]{2,1,0:T(2,128)(2,1)}, u32[]{:S(2)}, u32[]{:S(2)}) async-start(bf16[32,2,24576]{2,1,0:T(2,128)(2,1)} %reshape.318), calls=%async_computation.6 | async-start | bytes 6291456 | tf_op jit(solution)/shard_map/all_to_all | solution.py:187
  475.1 3.7 reduce.9
  478.8 5.4 reshape.322
  484.2 17.9 %all-to-all-done.6 = bf16[32,2,24576]{2,1,0:T(2,128)(2,1)} async-done(((bf16[32,2,24576]{2,1,0:T(2,128)(2,1)}), bf16[32,2,24576]{2,1,0:T(2,128)(2,1)}, u32[]{:S(2)}, u32[]{:S(2)}) %all-to-all-start.6) | async-done | bytes 3145760 | tf_op jit(solution)/shard_map/all_to_all | solution.py:187
  502.1 8.5 %all-to-all-start.10 = ((bf16[32,2,24576]{2,1,0:T(2,128)(2,1)}), bf16[32,2,24576]{2,1,0:T(2,128)(2,1)}, u32[]{:S(2)}, u32[]{:S(2)}) async-start(bf16[32,2,24576]{2,1,0:T(2,128)(2,1)} %reshape.322), calls=%async_computation.10 | async-start | bytes 6291456 | tf_op jit(solution)/shard_map/all_to_all | solution.py:193
  521.6 3.7 reduce.8
  525.3 5.4 reshape.320
  530.7 18.0 %all-to-all-done.10 = bf16[32,2,24576]{2,1,0:T(2,128)(2,1)} async-done(((bf16[32,2,24576]{2,1,0:T(2,128)(2,1)}), bf16[32,2,24576]{2,1,0:T(2,128)(2,1)}, u32[]{:S(2)}, u32[]{:S(2)}) %all-to-all-start.10) | async-done | bytes 3145760 | tf_op jit(solution)/shard_map/all_to_all | solution.py:193
  548.7 8.1 %all-to-all-start.8 = ((bf16[32,2,24576]{2,1,0:T(2,128)(2,1)}), bf16[32,2,24576]{2,1,0:T(2,128)(2,1)S(1)}, u32[]{:S(2)}, u32[]{:S(2)}) async-start(bf16[32,2,24576]{2,1,0:T(2,128)(2,1)} %reshape.320), calls=%async_computation.8 | async-start | bytes 6291456 | tf_op jit(solution)/shard_map/all_to_all | solution.py:190
  556.8 18.9 %reshape.323 = bf16[32,1,49152]{2,1,0:T(2,128)(2,1)} reshape(bf16[32,2,24576]{2,1,0:T(2,128)(2,1)} %all-to-all-done.10) | data formatting | bytes 6291456
  575.8 7.4 %convolution_convert_fusion.7 = bf16[16,49152]{1,0:T(8,128)(2,1)} fusion(bf16[32,1,49152]{2,1,0:T(2,128)(2,1)} %reshape.323, s32[16]{0:T(128)S(1)} %copy-done.26, pred[16]{0:T(512)(128)(4,1)S(1)} %copy-done.28), kind=kOutput, calls=%fused_computation.86 | convolution fusion | flops 51119104 | bytes 4718672 | tf_op jit(solution)/shard_map/dot_general | solution.py:44
  585.9 9.0 %all-to-all-done.8 = bf16[32,2,24576]{2,1,0:T(2,128)(2,1)S(1)} async-done(((bf16[32,2,24576]{2,1,0:T(2,128)(2,1)}), bf16[32,2,24576]{2,1,0:T(2,128)(2,1)S(1)}, u32[]{:S(2)}, u32[]{:S(2)}) %all-to-all-start.8) | async-done | bytes 3145760 | tf_op jit(solution)/shard_map/all_to_all | solution.py:190
  594.9 4.3 all-to-all-start.11
  599.2 12.5 %reshape.321 = bf16[32,1,49152]{2,1,0:T(2,128)(2,1)} reshape(bf16[32,2,24576]{2,1,0:T(2,128)(2,1)S(1)} %all-to-all-done.8) | data formatting | bytes 6291456
  611.7 6.3 convolution_convert_fusion.8
  619.6 18.9 %all-to-all-done.11 = bf16[8,256,384]{2,1,0:T(8,128)(2,1)} async-done(((bf16[8,256,384]{2,1,0:T(8,128)(2,1)}), bf16[8,256,384]{2,1,0:T(8,128)(2,1)}, u32[]{:S(2)}, u32[]{:S(2)}) %all-to-all-start.11) | async-done | bytes 1572896 | tf_op jit(solution)/shard_map/all_to_all | solution.py:203
  638.4 4.0 all-to-all-start.9
  642.4 18.9 %reshape.319 = bf16[32,1,49152]{2,1,0:T(2,128)(2,1)} reshape(bf16[32,2,24576]{2,1,0:T(2,128)(2,1)} %all-to-all-done.6) | data formatting | bytes 6291456
  661.4 6.3 convolution_convert_fusion.9
  669.3 13.3 %all-to-all-done.9 = bf16[8,256,384]{2,1,0:T(8,128)(2,1)S(1)} async-done(((bf16[8,256,384]{2,1,0:T(8,128)(2,1)}), bf16[8,256,384]{2,1,0:T(8,128)(2,1)S(1)}, u32[]{:S(2)}, u32[]{:S(2)}) %all-to-all-start.9) | async-done | bytes 1572896 | tf_op jit(solution)/shard_map/all_to_all | solution.py:202
  682.5 3.6 all-to-all-start.7
  694.6 31.9 %all-to-all-done.7 = bf16[8,256,384]{2,1,0:T(8,128)(2,1)S(1)} async-done(((bf16[8,256,384]{2,1,0:T(8,128)(2,1)}), bf16[8,256,384]{2,1,0:T(8,128)(2,1)S(1)}, u32[]{:S(2)}, u32[]{:S(2)}) %all-to-all-start.7) | async-done | bytes 1572896 | tf_op jit(solution)/shard_map/all_to_all | solution.py:201
  (376 shorter events, 185.0 us)
Async XLA Ops:
  0.6 11.3 %copy-start.19 = (bf16[256,3072]{1,0:T(8,128)(2,1)S(1)}, bf16[256,3072]{1,0:T(8,128)(2,1)}, u32[]{:S(2)}) copy-start(bf16[256,3072]{1,0:T(8,128)(2,1)} %param.9) | copy-start | bytes 4718596
  3.5 48.4 %all-to-all-start = ((bf16[256,8,384]{2,0,1:T(8,128)(2,1)}), bf16[256,8,384]{2,0,1:T(8,128)(2,1)S(1)}, u32[]{:S(2)}, u32[]{:S(2)}) async-start(bf16[256,8,384]{2,0,1:T(8,128)(2,1)} %bitcast.182), calls=%async_computation | async-start | bytes 3145728 | tf_op jit(solution)/shard_map/all_to_all | solution.py:154
  51.9 6.3 copy-start.16
  51.9 41.8 %all-to-all-start.2 = ((bf16[256,8,384]{2,0,1:T(8,128)(2,1)}), bf16[256,8,384]{2,0,1:T(8,128)(2,1)S(1)}, u32[]{:S(2)}, u32[]{:S(2)}) async-start(bf16[256,8,384]{2,0,1:T(8,128)(2,1)} %bitcast.252), calls=%async_computation.2 | async-start | bytes 3145728 | tf_op jit(solution)/shard_map/all_to_all | solution.py:155
  55.5 42.5 %copy-start.29 = (s32[512]{0:T(512)S(1)}, s32[512]{0:T(512)}, u32[]{:S(2)}) copy-start(s32[512]{0:T(512)} %param.12) | copy-start | bytes 6148
  93.7 44.7 %all-to-all-start.4 = ((bf16[256,8,384]{2,0,1:T(8,128)(2,1)}), bf16[256,8,384]{2,0,1:T(8,128)(2,1)}, u32[]{:S(2)}, u32[]{:S(2)}) async-start(bf16[256,8,384]{2,0,1:T(8,128)(2,1)} %bitcast.180), calls=%async_computation.4 | async-start | bytes 3145728 | tf_op jit(solution)/shard_map/all_to_all | solution.py:156
  98.4 96.2 %copy-start.25 = (s32[16]{0:T(128)}, s32[16]{0:T(128)S(1)}, u32[]{:S(2)}) copy-start(s32[16]{0:T(128)S(1)} %dynamic-slice_reduce_fusion) | copy-start | bytes 196
  98.7 95.9 %copy-start.27 = (pred[16]{0:T(512)(128)(4,1)}, pred[16]{0:T(512)(128)(4,1)S(1)}, u32[]{:S(2)}) copy-start(pred[16]{0:T(512)(128)(4,1)S(1)} %fusion.92) | copy-start | bytes 52
  138.4 45.6 %all-to-all-start.3 = ((bf16[32,2,24576]{2,1,0:T(2,128)(2,1)}), bf16[32,2,24576]{2,1,0:T(2,128)(2,1)}, u32[]{:S(2)}, u32[]{:S(2)}) async-start(bf16[32,2,24576]{2,1,0:T(2,128)(2,1)} %reshape.314), calls=%async_computation.3 | async-start | bytes 6291456 | tf_op jit(solution)/shard_map/all_to_all | solution.py:164
  160.3 32.6 %copy-start.17 = (bf16[256,8,384]{2,0,1:T(8,128)(2,1)S(1)}, bf16[256,8,384]{2,0,1:T(8,128)(2,1)}, u32[]{:S(2)}) copy-start(bf16[256,8,384]{2,0,1:T(8,128)(2,1)} %copy-done.16) | copy-start | bytes 4718596
  184.0 47.1 %all-to-all-start.5 = ((bf16[32,2,24576]{2,1,0:T(2,128)(2,1)}), bf16[32,2,24576]{2,1,0:T(2,128)(2,1)}, u32[]{:S(2)}, u32[]{:S(2)}) async-start(bf16[32,2,24576]{2,1,0:T(2,128)(2,1)} %reshape.316), calls=%async_computation.5 | async-start | bytes 6291456 | tf_op jit(solution)/shard_map/all_to_all | solution.py:167
  206.0 33.3 %copy-start.30 = (s32[1,5]{1,0:T(1,128)S(1)}, s32[1,5]{1,0:T(1,128)}, u32[]{:S(2)}) copy-start(s32[1,5]{1,0:T(1,128)} %param.13) | copy-start | bytes 64
  206.0 34.1 %copy-start.20 = (bf16[2048,384]{1,0:T(8,128)(2,1)S(1)}, bf16[2048,384]{1,0:T(8,128)(2,1)}, u32[]{:S(2)}) copy-start(bf16[2048,384]{1,0:T(8,128)(2,1)} %param.11) | copy-start | bytes 4718596
  231.1 74.6 %all-to-all-start.1 = ((bf16[32,2,24576]{2,1,0:T(2,128)(2,1)}), bf16[32,2,24576]{2,1,0:T(2,128)(2,1)}, u32[]{:S(2)}, u32[]{:S(2)}) async-start(bf16[32,2,24576]{2,1,0:T(2,128)(2,1)} %reshape.312), calls=%async_computation.1 | async-start | bytes 6291456 | tf_op jit(solution)/shard_map/all_to_all | solution.py:161
  341.6 8.1 %copy-start.4 = (bf16[2432,3,128]{2,0,1:T(8,128)(2,1)}, bf16[2432,3,128]{2,0,1:T(8,128)(2,1)S(1)}, u32[]{:S(2)}) copy-start(bf16[2432,3,128]{2,0,1:T(8,128)(2,1)S(1)} %get-tuple-element.524) | copy-start | bytes 5603332 | tf_op jit(solution)/shard_map/while
  345.4 3.1 copy-start.6
  362.2 3.9 copy-start.5
  362.2 3.9 copy-start.22
  362.2 3.8 copy-start.24
  362.2 3.8 copy-start.32
  366.1 8.1 %copy-start.4 = (bf16[2432,3,128]{2,0,1:T(8,128)(2,1)}, bf16[2432,3,128]{2,0,1:T(8,128)(2,1)S(1)}, u32[]{:S(2)}) copy-start(bf16[2432,3,128]{2,0,1:T(8,128)(2,1)S(1)} %get-tuple-element.524) | copy-start | bytes 5603332 | tf_op jit(solution)/shard_map/while
  369.9 3.1 copy-start.6
  382.9 3.0 copy-start
  386.7 3.9 copy-start.5
  386.7 3.9 copy-start.22
  386.7 3.8 copy-start.24
  386.8 3.8 copy-start.32
  390.6 8.1 %copy-start.4 = (bf16[2432,3,128]{2,0,1:T(8,128)(2,1)}, bf16[2432,3,128]{2,0,1:T(8,128)(2,1)S(1)}, u32[]{:S(2)}) copy-start(bf16[2432,3,128]{2,0,1:T(8,128)(2,1)S(1)} %get-tuple-element.524) | copy-start | bytes 5603332 | tf_op jit(solution)/shard_map/while
  394.4 3.1 copy-start.6
  407.4 3.0 copy-start
  411.3 3.9 copy-start.5
  411.3 3.9 copy-start.22
  411.3 3.8 copy-start.24
  411.3 3.8 copy-start.32
  415.2 8.1 %copy-start.4 = (bf16[2432,3,128]{2,0,1:T(8,128)(2,1)}, bf16[2432,3,128]{2,0,1:T(8,128)(2,1)S(1)}, u32[]{:S(2)}) copy-start(bf16[2432,3,128]{2,0,1:T(8,128)(2,1)S(1)} %get-tuple-element.524) | copy-start | bytes 5603332 | tf_op jit(solution)/shard_map/while
  419.0 3.1 copy-start.6
  435.8 3.9 copy-start.5
  435.8 3.9 copy-start.22
  435.8 3.8 copy-start.24
  435.8 3.8 copy-start.32
  456.5 45.5 %all-to-all-start.6 = ((bf16[32,2,24576]{2,1,0:T(2,128)(2,1)}), bf16[32,2,24576]{2,1,0:T(2,128)(2,1)}, u32[]{:S(2)}, u32[]{:S(2)}) async-start(bf16[32,2,24576]{2,1,0:T(2,128)(2,1)} %reshape.318), calls=%async_computation.6 | async-start | bytes 6291456 | tf_op jit(solution)/shard_map/all_to_all | solution.py:187
  502.1 46.6 %all-to-all-start.10 = ((bf16[32,2,24576]{2,1,0:T(2,128)(2,1)}), bf16[32,2,24576]{2,1,0:T(2,128)(2,1)}, u32[]{:S(2)}, u32[]{:S(2)}) async-start(bf16[32,2,24576]{2,1,0:T(2,128)(2,1)} %reshape.322), calls=%async_computation.10 | async-start | bytes 6291456 | tf_op jit(solution)/shard_map/all_to_all | solution.py:193
  548.7 46.2 %all-to-all-start.8 = ((bf16[32,2,24576]{2,1,0:T(2,128)(2,1)}), bf16[32,2,24576]{2,1,0:T(2,128)(2,1)S(1)}, u32[]{:S(2)}, u32[]{:S(2)}) async-start(bf16[32,2,24576]{2,1,0:T(2,128)(2,1)} %reshape.320), calls=%async_computation.8 | async-start | bytes 6291456 | tf_op jit(solution)/shard_map/all_to_all | solution.py:190
  556.8 19.0 %copy-start.26 = (s32[16]{0:T(128)S(1)}, s32[16]{0:T(128)}, u32[]{:S(2)}) copy-start(s32[16]{0:T(128)} %copy-done.25) | copy-start | bytes 196
  556.8 19.0 %copy-start.28 = (pred[16]{0:T(512)(128)(4,1)S(1)}, pred[16]{0:T(512)(128)(4,1)}, u32[]{:S(2)}) copy-start(pred[16]{0:T(512)(128)(4,1)} %copy-done.27) | copy-start | bytes 52
  594.9 43.5 %all-to-all-start.11 = ((bf16[8,256,384]{2,1,0:T(8,128)(2,1)}), bf16[8,256,384]{2,1,0:T(8,128)(2,1)}, u32[]{:S(2)}, u32[]{:S(2)}) async-start(bf16[8,256,384]{2,1,0:T(8,128)(2,1)} %all_to_all.161), calls=%async_computation.11 | async-start | bytes 3145728 | tf_op jit(solution)/shard_map/all_to_all | solution.py:203
  638.4 44.1 %all-to-all-start.9 = ((bf16[8,256,384]{2,1,0:T(8,128)(2,1)}), bf16[8,256,384]{2,1,0:T(8,128)(2,1)S(1)}, u32[]{:S(2)}, u32[]{:S(2)}) async-start(bf16[8,256,384]{2,1,0:T(8,128)(2,1)} %all_to_all.154), calls=%async_computation.9 | async-start | bytes 3145728 | tf_op jit(solution)/shard_map/all_to_all | solution.py:202
  682.5 43.9 %all-to-all-start.7 = ((bf16[8,256,384]{2,1,0:T(8,128)(2,1)}), bf16[8,256,384]{2,1,0:T(8,128)(2,1)S(1)}, u32[]{:S(2)}, u32[]{:S(2)}) async-start(bf16[8,256,384]{2,1,0:T(8,128)(2,1)} %all_to_all.147), calls=%async_computation.7 | async-start | bytes 3145728 | tf_op jit(solution)/shard_map/all_to_all | solution.py:201
  (63 other events, 105.7 us)
where the time goes:
time: 742 us; the launch traced here: 728 us
  local copies, waits for them, and re-layouts  270 us (36%)
  waiting for transfers between devices  258 us (35%)
  matrix products  84.8 us (11%)
  starting transfers between devices  77 us (10%)
  other arithmetic  34.1 us (5%)
    unnamed x40, local copies, waits for them, and re-layouts  152 us
    dot_general x12, matrix products, select_tiles(): jnp.dot(tile_table, flat_tiles, preferred_element_type=jnp.float32)  55.1 us
    all_to_all x1, waiting for transfers between devices, shards(): lax.all_to_all(query_in, 'ulysses', split_axis=1, concat_axis=0, tiled=True)  38.6 us
    all_to_all x1, waiting for transfers between devices, shards(): lax.all_to_all(key_in, 'ulysses', split_axis=1, concat_axis=0, tiled=True)  35.4 us
    all_to_all x1, waiting for transfers between devices, shards(): lax.all_to_all(query_anchor, 'ulysses', split_axis=0, concat_axis=1, tile...  31.9 us
    all_to_all x1, waiting for transfers between devices, shards(): lax.all_to_all(value_in, 'ulysses', split_axis=1, concat_axis=0, tiled=True)  26 us
    all_to_all x1, waiting for transfers between devices, shards(): lax.all_to_all(select_tiles(send_table, value_row), 'dp', split_axis=0, c...  25.1 us
    while x176, local copies, waits for them, and re-layouts  24.8 us
  transfers between devices with their start and end apart: 12, of which 11 were waited for; matrix products, arithmetic and copies ran while one was open for 32% of the time, Pallas kernels for 0%

commit v1 on v0

v1 whole, which is shorter than its diff:
```python
import functools
import jax
import jax.numpy as jnp
from jax import lax
from jax.experimental import pallas as pl
from jax.experimental.pallas import tpu as pltpu
from jax.sharding import PartitionSpec as P

HEAD_DIM = 128
TILE = 128
DOC_MOST = 4
ROW_TOK = 2048
TILES = 16
DOCS = 5
PARTS = 3
LOG2E = 1.4426950408889634
DEST, SOURCE, ZPOS, DOCLEN = 0, 16, 32, 33

ANY = pl.BlockSpec(memory_space=pl.ANY)
SMEM = pl.BlockSpec(memory_space=pltpu.SMEM)


def run_copies(copies):
    for copy in copies:
        copy.start()
    for copy in copies:
        copy.wait()


def split_kernel(chunk, n_z, heads, n_after, tab, q, k, v, *rest):
    outs, sem = rest[n_after:-1], rest[-1]
    copies = []
    for shift in range(n_z):
        group = lax.rem(tab[ZPOS] + shift, n_z)
        col = pl.multiple_of((group * heads + chunk) * HEAD_DIM, HEAD_DIM)
        for part, src in enumerate((q, k, v)):
            copies.append(
                pltpu.make_async_copy(
                    src.at[:, pl.ds(col, HEAD_DIM)],
                    outs[shift].at[part],
                    sem.at[shift * PARTS + part],
                )
            )
    run_copies(copies)


def split_heads(chunk, n_z, heads, tab, q, k, v, after):
    rows = q.shape[0]
    piece = jax.ShapeDtypeStruct((PARTS, rows, HEAD_DIM), q.dtype)
    return pl.pallas_call(
        functools.partial(split_kernel, chunk, n_z, heads, len(after)),
        out_shape=[piece] * n_z,
        in_specs=[SMEM] + [ANY] * (3 + len(after)),
        out_specs=[ANY] * n_z,
        scratch_shapes=[pltpu.SemaphoreType.DMA((n_z * PARTS,))],
        cost_estimate=pl.CostEstimate(flops=0, bytes_accessed=4 << 20, transcendentals=0),
    )(tab, q, k, v, *after)


def pack_kernel(n_z, per, tab, *rest):
    pieces, send, sem = rest[:n_z], rest[n_z], rest[-1]
    copies = []
    for shift in range(n_z):
        origin = lax.rem(tab[ZPOS] + n_z - shift, n_z)
        for i in range(per):
            dest = tab[DEST + origin * per + i]
            copies.append(
                pltpu.make_async_copy(
                    pieces[shift].at[:, pl.ds(i * TILE, TILE), :],
                    send.at[dest],
                    sem.at[shift * per + i],
                )
            )
    run_copies(copies)


def pack_tiles(n_dp, tab, pieces):
    n_z = len(pieces)
    per = TILES // n_z
    return pl.pallas_call(
        functools.partial(pack_kernel, n_z, per),
        out_shape=jax.ShapeDtypeStruct((n_dp, PARTS, TILE, HEAD_DIM), pieces[0].dtype),
        in_specs=[SMEM] + [ANY] * n_z,
        out_specs=ANY,
        scratch_shapes=[pltpu.SemaphoreType.DMA((TILES,))],
        cost_estimate=pl.CostEstimate(flops=0, bytes_accessed=4 << 20, transcendentals=0),
    )(tab, *pieces)


def unpack_kernel(n_z, per, tab, got, *rest):
    pieces, sem = rest[:n_z], rest[-1]
    copies = []
    for shift in range(n_z):
        target = lax.rem(tab[ZPOS] + shift, n_z)
        for i in range(per):
            dest = tab[DEST + target * per + i]
            copies.append(
                pltpu.make_async_copy(
                    got.at[dest],
                    pieces[shift].at[:, pl.ds(i * TILE, TILE), :],
                    sem.at[shift * per + i],
                )
            )
    run_copies(copies)


def unpack_tiles(n_z, tab, got):
    per = TILES // n_z
    piece = jax.ShapeDtypeStruct((PARTS, per * TILE, HEAD_DIM), got.dtype)
    return pl.pallas_call(
        functools.partial(unpack_kernel, n_z, per),
        out_shape=[piece] * n_z,
        in_specs=[SMEM, ANY],
        out_specs=[ANY] * n_z,
        scratch_shapes=[pltpu.SemaphoreType.DMA((TILES,))],
        cost_estimate=pl.CostEstimate(flops=0, bytes_accessed=4 << 20, transcendentals=0),
    )(tab, got)


def join_kernel(chunk, n_z, heads, n_prev, tab, *rest):
    pieces, outs, sem = rest[:n_z], rest[n_z + n_prev : -1], rest[-1]
    copies = []
    for shift in range(n_z):
        group = lax.rem(tab[ZPOS] + n_z - shift, n_z)
        col = pl.multiple_of((group * heads + chunk) * HEAD_DIM, HEAD_DIM)
        for part in range(PARTS):
            copies.append(
                pltpu.make_async_copy(
                    pieces[shift].at[part],
                    outs[part].at[:, pl.ds(col, HEAD_DIM)],
                    sem.at[shift * PARTS + part],
                )
            )
    run_copies(copies)


def join_heads(chunk, n_z, heads, tab, pieces, prev):
    rows = pieces[0].shape[1]
    out = jax.ShapeDtypeStruct((rows, n_z * heads * HEAD_DIM), pieces[0].dtype)
    return pl.pallas_call(
        functools.partial(join_kernel, chunk, n_z, heads, len(prev)),
        out_shape=[out] * PARTS,
        in_specs=[SMEM] + [ANY] * (n_z + len(prev)),
        out_specs=[ANY] * PARTS,
        scratch_shapes=[pltpu.SemaphoreType.DMA((n_z * PARTS,))],
        input_output_aliases={1 + n_z + i: i for i in range(len(prev))},
        cost_estimate=pl.CostEstimate(flops=0, bytes_accessed=4 << 20, transcendentals=0),
    )(tab, *pieces, *prev)


def attend_kernel(n_prev, tab, grad, got, *rest):
    att, back, tiles, grads, in_sem, out_sem = rest[n_prev:]
    scale = HEAD_DIM ** (-0.5)
    nt = (((1,), (1,)), ((), ()))
    tn = (((0,), (0,)), ((), ()))
    nn = (((1,), (0,)), ((), ()))

    def dot(a, b, dims):
        return lax.dot_general(a, b, dims, preferred_element_type=jnp.float32)

    run_copies(
        [
            pltpu.make_async_copy(
                got.at[tab[SOURCE + t]], tiles.at[:, pl.ds(t * TILE, TILE), :], in_sem.at[t]
            )
            for t in range(TILES)
        ]
    )

    def document(first, count):
        extent = count * TILE
        rows = pl.ds(pl.multiple_of(first * TILE, TILE), extent)
        q, k, v = tiles[0, rows, :], tiles[1, rows, :], tiles[2, rows, :]
        g = grad[rows, :]
        scores = dot(q, k, nt)
        later = lax.broadcasted_iota(jnp.int32, (extent, extent), 0)
        earlier = lax.broadcasted_iota(jnp.int32, (extent, extent), 1)
        scores = jnp.where(later >= earlier, scores, -jnp.inf)
        top = jnp.max(scores, axis=1, keepdims=True)
        weights = jnp.exp2((scores - top) * (scale * LOG2E))
        probs = weights * (1.0 / jnp.sum(weights, axis=1, keepdims=True))
        low = probs.astype(jnp.bfloat16)
        attended = dot(low, v, nn).astype(jnp.bfloat16)
        att[rows, :] = attended
        delta = jnp.sum(
            g.astype(jnp.float32) * attended.astype(jnp.float32), axis=1, keepdims=True
        )
        grads[2, rows, :] = dot(low, g, tn).astype(jnp.bfloat16)
        grad_scores = (probs * (dot(g, v, nt) - delta)).astype(jnp.bfloat16)
        grads[0, rows, :] = (dot(grad_scores, k, nn) * scale).astype(jnp.bfloat16)
        grads[1, rows, :] = (dot(grad_scores, q, tn) * scale).astype(jnp.bfloat16)

    def step(j, first):
        count = tab[DOCLEN + j]
        for size in range(1, DOC_MOST + 1):
            pl.when(count == size)(functools.partial(document, first, size))
        return first + count

    lax.fori_loop(0, DOCS, step, jnp.int32(0))
    run_copies(
        [
            pltpu.make_async_copy(
                grads.at[:, pl.ds(t * TILE, TILE), :], back.at[tab[SOURCE + t]], out_sem.at[t]
            )
            for t in range(TILES)
        ]
    )


def attend(chunk, heads, tab, grad_out, got, prev):
    column = pl.BlockSpec((ROW_TOK, HEAD_DIM), lambda i: (0, chunk))
    return pl.pallas_call(
        functools.partial(attend_kernel, len(prev)),
        grid=(1,),
        out_shape=[
            jax.ShapeDtypeStruct(grad_out.shape, grad_out.dtype),
            jax.ShapeDtypeStruct(got.shape, got.dtype),
        ],
        in_specs=[SMEM, column, ANY] + [ANY] * len(prev),
        out_specs=[column, ANY],
        scratch_shapes=[
            pltpu.VMEM((PARTS, ROW_TOK, HEAD_DIM), jnp.bfloat16),
            pltpu.VMEM((PARTS, ROW_TOK, HEAD_DIM), jnp.bfloat16),
            pltpu.SemaphoreType.DMA((TILES,)),
            pltpu.SemaphoreType.DMA((TILES,)),
        ],
        input_output_aliases={3 + i: i for i in range(len(prev))},
        compiler_params=pltpu.CompilerParams(vmem_limit_bytes=40 << 20),
        cost_estimate=pl.CostEstimate(
            flops=2 << 30, bytes_accessed=8 << 20, transcendentals=1 << 20
        ),
    )(tab, grad_out, got, *prev)


def shift_by(pieces, n_z):
    moved = [pieces[0]]
    for shift in range(1, n_z):
        moved.append(
            lax.ppermute(pieces[shift], "ulysses", [(i, (i + shift) % n_z) for i in range(n_z)])
        )
    return moved


def shards(query_in, key_in, value_in, grad_out, packing, doc_tiles):
    n_dp = lax.axis_size("dp")
    n_z = lax.axis_size("ulysses")
    row_index = lax.axis_index("dp")
    heads = grad_out.shape[1] // HEAD_DIM
    dest = lax.dynamic_slice_in_dim(packing, row_index * TILES, TILES) // TILES
    place = row_index * TILES + jnp.arange(TILES, dtype=jnp.int32)
    source_row = jnp.arange(packing.shape[0], dtype=jnp.int32) // TILES
    source = jnp.sum(
        jnp.where(packing[None, :] == place[:, None], source_row[None, :], 0),
        axis=1,
        dtype=jnp.int32,
    )
    tab = jnp.concatenate(
        [dest, source, lax.axis_index("ulysses")[None].astype(jnp.int32), doc_tiles[0]]
    )

    got, sent = [], ()
    for chunk in range(heads):
        pieces = split_heads(chunk, n_z, heads, tab, query_in, key_in, value_in, sent)
        send = pack_tiles(n_dp, tab, shift_by(pieces, n_z))
        sent = (send,)
        got.append(lax.all_to_all(send, "dp", split_axis=0, concat_axis=0, tiled=True))

    back, prev = [], ()
    for chunk in range(heads):
        attended, home = attend(chunk, heads, tab, grad_out, got[chunk], prev)
        prev = (attended,)
        back.append(lax.all_to_all(home, "dp", split_axis=0, concat_axis=0, tiled=True))

    grads = ()
    for chunk in range(heads):
        pieces = shift_by(unpack_tiles(n_z, tab, back[chunk]), n_z)
        grads = tuple(join_heads(chunk, n_z, heads, tab, pieces, grads))
    return (attended,) + grads


def solution(mesh):
    in_specs = (
        P(("dp", "ulysses"), None),
        P(("dp", "ulysses"), None),
        P(("dp", "ulysses"), None),
        P("dp", "ulysses"),
        P(),
        P("dp", None),
    )
    out_specs = (
        P("dp", "ulysses"),
        P(("dp", "ulysses"), None),
        P(("dp", "ulysses"), None),
        P(("dp", "ulysses"), None),
    )
    return jax.shard_map(shards, mesh=mesh, in_specs=in_specs, out_specs=out_specs, check_vma=False)
```

time: 742 us -> 969 us (1.31)
  Pallas kernels: 0 us -> 624 us
  local copies, waits for them, and re-layouts: 270 us -> 6.24 us
  matrix products: 84.8 us -> 0 us
  waiting for transfers between devices: 258 us -> 178 us
  starting transfers between devices: 77 us -> 146 us
  other arithmetic: 34.1 us -> 2.92 us
    pallas_call x0 -> x15, Pallas kernels: none -> 624 us  [the longest x3 149 us: split_heads(): pl.pallas_call(functools.partial(split_kernel, chunk, n_z, heads, len(aft...]
    all_to_all x12 -> x6, waiting for transfers between devices: 258 us -> 82.2 us  [the longest x3 56.1 us: shards(): lax.all_to_all(home, 'dp', split_axis=0, concat_axis=0, tiled=True)]
    unnamed x40 -> x60, local copies, waits for them, and re-layouts: 152 us -> 6.24 us
    ppermute x0 -> x42, starting transfers between devices: none -> 98.6 us  [shift_by(): lax.ppermute(pieces[shift], 'ulysses', [(i, (i + shift) % n_z) for i in r...]
    ppermute x0 -> x42, waiting for transfers between devices: none -> 95.5 us  [shift_by(): lax.ppermute(pieces[shift], 'ulysses', [(i, (i + shift) % n_z) for i in r...]
    dot_general x33 -> x0, matrix products: 72.8 us -> none  [the longest x12 55.1 us: select_tiles(): jnp.dot(tile_table, flat_tiles, preferred_element_type=jnp.float32)]
    all_to_all x12 -> x6, starting transfers between devices: 77 us -> 47.8 us  [the longest x3 25 us: shards(): lax.all_to_all(home, 'dp', split_axis=0, concat_axis=0, tiled=True)]
    while x177 -> x0, local copies, waits for them, and re-layouts: 27.5 us -> none
  transfers between devices with their start and end apart: 12 -> 48, of which waited for: 11 -> 21; matrix products, arithmetic and copies ran while one was open for 32% -> 0% of each run, Pallas kernels for 0% -> 50%
where the time goes in v1:
time: 969 us; the launch traced here: 959 us
  Pallas kernels  624 us (64%)
  waiting for transfers between devices  178 us (18%)
  starting transfers between devices  146 us (15%)
    pallas_call x3, Pallas kernels, split_heads(): pl.pallas_call(functools.partial(split_kernel, chunk, n_z, heads, len(aft...  149 us
    pallas_call x3, Pallas kernels, join_heads(): pl.pallas_call(functools.partial(join_kernel, chunk, n_z, heads, len(prev...  149 us
    pallas_call x3, Pallas kernels, unpack_tiles(): pl.pallas_call(functools.partial(unpack_kernel, n_z, per), out_shape=[pie...  149 us
    pallas_call x3, Pallas kernels, pack_tiles(): pl.pallas_call(functools.partial(pack_kernel, n_z, per), out_shape=jax.Sh...  149 us
    ppermute x42, starting transfers between devices, shift_by(): lax.ppermute(pieces[shift], 'ulysses', [(i, (i + shift) % n_z) for i in r...  98.6 us
    ppermute x42, waiting for transfers between devices, shift_by(): lax.ppermute(pieces[shift], 'ulysses', [(i, (i + shift) % n_z) for i in r...  95.5 us
    all_to_all x3, waiting for transfers between devices, shards(): lax.all_to_all(home, 'dp', split_axis=0, concat_axis=0, tiled=True)  56.1 us
    pallas_call x3, Pallas kernels, attend(): pl.pallas_call(functools.partial(attend_kernel, len(prev)), grid=(1,), ou...  29.1 us
  transfers between devices with their start and end apart: 48, of which 21 were waited for; matrix products, arithmetic and copies ran while one was open for 0% of the time, Pallas kernels for 50%

profile of v1, /device:TPU:6, one launch (start us, length us, event | category | flops | bytes accessed | tf_op | source)
XLA Modules:
  0.0 959.2 jit_solution(16202012166415962989)
XLA Ops:
  3.6 49.6 %shard_map.93 = (bf16[3,256,128]{2,1,0:T(8,128)(2,1)}, bf16[3,256,128]{2,1,0:T(8,128)(2,1)}, bf16[3,256,128]{2,1,0:T(8,128)(2,1)}, bf16[3,256,128]{2,1,0:T(8,128...) custom-call(s32[38]{0:T(128)} %pad_add_fusion.tab, ...), custom_call_target="tpu_custom_call" | custom-call | bytes 4194304 | tf_op jit(solution)/shard_map/pallas_call | solution.py:50
  58.5 4.0 collective-permute-start.2
  63.1 4.9 collective-permute-start.4
  68.0 4.0 collective-permute-start.5
  72.0 4.4 collective-permute-done.1.rest_2_
  79.4 10.3 %collective-permute-done.2.rest_3_ = bf16[3,256,128]{2,1,0:T(8,128)(2,1)S(1)} collective-permute-done((bf16[3,256,128]{2,1,0:T(8,128)(2,1)}, bf16[3,256,128]{2,1,0:T(8,128)(2,1)S(1)}, u32[]{:S(2)}, u32[]{:S(2)}) %collective-permute-start.2) | collective-permute-done | bytes 196640 | tf_op jit(solution)/shard_map/ppermute | solution.py:239
  90.9 5.6 collective-permute-done.5.rest_6_
  99.2 49.6 %shard_map.94.rest_0_ = bf16[32,3,128,128]{3,2,1,0:T(8,128)(2,1)} custom-call(s32[38]{0:T(128)} %pad_add_fusion.tab, bf16[3,256,128]{2,1,0:T(8,128)(2,1)} %get-tuple-element.67.rest_0_, bf16[3,256,128]{2,1,0:T(8,128)(2,1)} %copy-done.17, bf16[3,256,128]{2,1,0:T(8,128)(2,1)} %copy-done.20, bf16[3,256,128]{2,1,0:T(8,128)(2,1)} %copy-done.23, ...), custom_call_target="tpu_custom_call" | custom-call | bytes 4194304 | tf_op jit(solution)/shard_map/pallas_call | solution.py:80
  148.8 7.6 all-to-all-start.2
  156.4 49.6 %shard_map.95 = (bf16[3,256,128]{2,1,0:T(8,128)(2,1)}, bf16[3,256,128]{2,1,0:T(8,128)(2,1)}, bf16[3,256,128]{2,1,0:T(8,128)(2,1)}, bf16[3,256,128]{2,1,0:T(8,128...) custom-call(s32[38]{0:T(128)} %pad_add_fusion.tab, ...), custom_call_target="tpu_custom_call" | custom-call | bytes 4194304 | tf_op jit(solution)/shard_map/pallas_call | solution.py:50
  206.0 3.7 collective-permute-start.7
  211.4 4.8 collective-permute-start.10
  220.0 10.2 %collective-permute-done.8.rest_2_ = bf16[3,256,128]{2,1,0:T(8,128)(2,1)S(1)} collective-permute-done((bf16[3,256,128]{2,1,0:T(8,128)(2,1)}, bf16[3,256,128]{2,1,0:T(8,128)(2,1)S(1)}, u32[]{:S(2)}, u32[]{:S(2)}) %collective-permute-start.8) | collective-permute-done | bytes 196640 | tf_op jit(solution)/shard_map/ppermute | solution.py:239
  230.2 7.2 collective-permute-done.9.rest_3_
  237.4 6.2 collective-permute-done.10.rest_4_
  247.0 4.2 collective-permute-done.13.rest_7_
  251.2 49.6 %shard_map.96.rest_0_ = bf16[32,3,128,128]{3,2,1,0:T(8,128)(2,1)} custom-call(s32[38]{0:T(128)} %pad_add_fusion.tab, bf16[3,256,128]{2,1,0:T(8,128)(2,1)} %get-tuple-element.75.rest_0_, bf16[3,256,128]{2,1,0:T(8,128)(2,1)} %copy-done.18, bf16[3,256,128]{2,1,0:T(8,128)(2,1)} %copy-done.21, bf16[3,256,128]{2,1,0:T(8,128)(2,1)} %collective-permute-done.9.rest_3_, ...), custom_call_target="tpu_custom_call" | custom-call | bytes 4194304 | tf_op jit(solution)/shard_map/pallas_call | solution.py:80
  300.8 7.8 all-to-all-start.1
  308.6 49.6 %shard_map.97 = (bf16[3,256,128]{2,1,0:T(8,128)(2,1)}, bf16[3,256,128]{2,1,0:T(8,128)(2,1)}, bf16[3,256,128]{2,1,0:T(8,128)(2,1)}, bf16[3,256,128]{2,1,0:T(8,128...) custom-call(s32[38]{0:T(128)} %pad_add_fusion.tab, ...), custom_call_target="tpu_custom_call" | custom-call | bytes 4194304 | tf_op jit(solution)/shard_map/pallas_call | solution.py:50
  360.7 3.6 collective-permute-start.16
  365.5 4.4 collective-permute-start.18
  372.8 5.1 collective-permute-done.15.rest_2_
  378.0 10.8 %collective-permute-done.16.rest_3_ = bf16[3,256,128]{2,1,0:T(8,128)(2,1)} collective-permute-done((bf16[3,256,128]{2,1,0:T(8,128)(2,1)}, bf16[3,256,128]{2,1,0:T(8,128)(2,1)}, u32[]{:S(2)}, u32[]{:S(2)}) %collective-permute-start.16) | collective-permute-done | bytes 196640 | tf_op jit(solution)/shard_map/ppermute | solution.py:239
  388.8 8.4 collective-permute-done.17.rest_4_
  401.2 49.6 %shard_map.98 = bf16[32,3,128,128]{3,2,1,0:T(8,128)(2,1)} custom-call(s32[38]{0:T(128)} %pad_add_fusion.tab, bf16[3,256,128]{2,1,0:T(8,128)(2,1)} %get-tuple-element.83.rest_0_, bf16[3,256,128]{2,1,0:T(8,128)(2,1)} %copy-done.19, bf16[3,256,128]{2,1,0:T(8,128)(2,1)} %copy-done.22, bf16[3,256,128]{2,1,0:T(8,128)(2,1)} %collective-permute-done.16.rest_3_, ...), custom_call_target="tpu_custom_call" | custom-call | bytes 4194304 | tf_op jit(solution)/shard_map/pallas_call | solution.py:80
  450.8 7.4 all-to-all-start
  459.7 8.9 shard_map.99
  470.2 26.1 %all-to-all-done.got = bf16[32,3,128,128]{3,2,1,0:T(8,128)(2,1)} async-done(((bf16[32,3,128,128]{3,2,1,0:T(8,128)(2,1)}), bf16[32,3,128,128]{3,2,1,0:T(8,128)(2,1)}, u32[]{:S(2)}, u32[]{:S(2)}) %all-to-all-start) | async-done | bytes 3145760 | tf_op jit(solution)/shard_map/all_to_all | solution.py:266
  496.3 9.0 all-to-all-start.5
  505.3 10.1 %shard_map.100 = (bf16[2048,384]{1,0:T(8,128)(2,1)}, bf16[32,3,128,128]{3,2,1,0:T(8,128)(2,1)}) custom-call(s32[38]{0:T(128)S(1)} %copy-done.1, bf16[2048,384]{1,0:T(8,128)(2,1)S(1)} %copy-done.3, bf16[32,3,128,128]{3,2,1,0:T(8,128)(2,1)} %all-to-all-done.1.got, bf16[2048,384]{1,0:T(8,128)(2,1)} %get-tuple-element.91.rest_0_), custom_call_target="tpu_custom_call", output_to_operand_aliasing={{0}: (3, {})} | custom-call | flops 2147483648 | bytes 8388608 | tf_op jit(solution)/shard_map/pallas_call | solution.py:212
  515.4 28.1 %all-to-all-done.5.got = bf16[32,3,128,128]{3,2,1,0:T(8,128)(2,1)} async-done(((bf16[32,3,128,128]{3,2,1,0:T(8,128)(2,1)}), bf16[32,3,128,128]{3,2,1,0:T(8,128)(2,1)}, u32[]{:S(2)}, u32[]{:S(2)}) %all-to-all-start.5) | async-done | bytes 3145760 | tf_op jit(solution)/shard_map/all_to_all | solution.py:272
  543.5 8.2 all-to-all-start.4
  551.7 10.1 %shard_map.101 = (bf16[2048,384]{1,0:T(8,128)(2,1)}, bf16[32,3,128,128]{3,2,1,0:T(8,128)(2,1)}) custom-call(s32[38]{0:T(128)S(1)} %copy-done.1, bf16[2048,384]{1,0:T(8,128)(2,1)S(1)} %copy-done.3, bf16[32,3,128,128]{3,2,1,0:T(8,128)(2,1)} %all-to-all-done.got, bf16[2048,384]{1,0:T(8,128)(2,1)} %get-tuple-element.92.rest_0_), custom_call_target="tpu_custom_call", output_to_operand_aliasing={{0}: (3, {})} | custom-call | flops 2147483648 | bytes 8388608 | tf_op jit(solution)/shard_map/pallas_call | solution.py:212
  561.8 28.0 %all-to-all-done.4.got = bf16[32,3,128,128]{3,2,1,0:T(8,128)(2,1)} async-done(((bf16[32,3,128,128]{3,2,1,0:T(8,128)(2,1)}), bf16[32,3,128,128]{3,2,1,0:T(8,128)(2,1)}, u32[]{:S(2)}, u32[]{:S(2)}) %all-to-all-start.4) | async-done | bytes 3145760 | tf_op jit(solution)/shard_map/all_to_all | solution.py:272
  589.8 7.8 all-to-all-start.3
  597.6 49.6 %shard_map.104 = (bf16[3,256,128]{2,1,0:T(8,128)(2,1)}, bf16[3,256,128]{2,1,0:T(8,128)(2,1)}, bf16[3,256,128]{2,1,0:T(8,128)(2,1)}, bf16[3,256,128]{2,1,0:T(8,12...) custom-call(s32[38]{0:T(128)} %pad_add_fusion.tab, ...), custom_call_target="tpu_custom_call" | custom-call | bytes 4194304 | tf_op jit(solution)/shard_map/pallas_call | solution.py:110
  652.5 4.7 collective-permute-start.38
  661.1 49.6 %shard_map.103 = (bf16[3,256,128]{2,1,0:T(8,128)(2,1)}, bf16[3,256,128]{2,1,0:T(8,128)(2,1)}, bf16[3,256,128]{2,1,0:T(8,128)(2,1)}, bf16[3,256,128]{2,1,0:T(8,12...) custom-call(s32[38]{0:T(128)} %pad_add_fusion.tab, ...), custom_call_target="tpu_custom_call" | custom-call | bytes 4194304 | tf_op jit(solution)/shard_map/pallas_call | solution.py:110
  714.3 4.2 collective-permute-start.30
  721.3 49.6 %shard_map.102 = (bf16[3,256,128]{2,1,0:T(8,128)(2,1)}, bf16[3,256,128]{2,1,0:T(8,128)(2,1)}, bf16[3,256,128]{2,1,0:T(8,128)(2,1)}, bf16[3,256,128]{2,1,0:T(8,12...) custom-call(s32[38]{0:T(128)} %pad_add_fusion.tab, ...), custom_call_target="tpu_custom_call" | custom-call | bytes 4194304 | tf_op jit(solution)/shard_map/pallas_call | solution.py:110
  774.4 3.9 collective-permute-start.33
  780.4 8.5 collective-permute-done.32.rest_5_
  788.9 6.4 collective-permute-start.23
  795.5 5.4 collective-permute-start.24
  800.9 3.6 collective-permute-done.34.rest_7_
  808.8 49.6 %shard_map.105 = (bf16[256,3072]{1,0:T(8,128)(2,1)}, bf16[256,3072]{1,0:T(8,128)(2,1)}, bf16[256,3072]{1,0:T(8,128)(2,1)}) custom-call(s32[38]{0:T(128)} %pad_add_fusion.tab, bf16[3,256,128]{2,1,0:T(8,128)(2,1)} %get-tuple-element.113.rest_0_, bf16[3,256,128]{2,1,0:T(8,128)(2,1)} %collective-permute-done.35.rest_1_, bf16[3,256,128]{2,1,0:T(8,128)(2,1)} %copy-done.28, ...), custom_call_target="tpu_custom_call" | custom-call | bytes 4194304 | tf_op jit(solution)/shard_map/pallas_call | solution.py:140
  858.5 49.6 %shard_map.106 = (bf16[256,3072]{1,0:T(8,128)(2,1)}, bf16[256,3072]{1,0:T(8,128)(2,1)}, bf16[256,3072]{1,0:T(8,128)(2,1)}) custom-call(s32[38]{0:T(128)} %pad_add_fusion.tab, bf16[3,256,128]{2,1,0:T(8,128)(2,1)} %get-tuple-element.104.rest_0_, bf16[3,256,128]{2,1,0:T(8,128)(2,1)} %copy-done.5, ...), custom_call_target="tpu_custom_call", output_to_operand_aliasing={{0}: (9, {}), {1}: (10, {}), {2}: (11, {})} | custom-call | bytes 4194304 | tf_op jit(solution)/shard_map/pallas_call | solution.py:140
  909.1 49.6 %shard_map.107 = (bf16[256,3072]{1,0:T(8,128)(2,1)}, bf16[256,3072]{1,0:T(8,128)(2,1)}, bf16[256,3072]{1,0:T(8,128)(2,1)}) custom-call(s32[38]{0:T(128)} %pad_add_fusion.tab, bf16[3,256,128]{2,1,0:T(8,128)(2,1)} %get-tuple-element.95.rest_0_, bf16[3,256,128]{2,1,0:T(8,128)(2,1)} %copy-done.7, ...), custom_call_target="tpu_custom_call", output_to_operand_aliasing={{0}: (9, {}), {1}: (10, {}), {2}: (11, {})} | custom-call | bytes 4194304 | tf_op jit(solution)/shard_map/pallas_call | solution.py:140
  (128 shorter events, 64.7 us)
Async XLA Ops:
  53.2 14.8 %collective-permute-start = (bf16[3,256,128]{2,1,0:T(8,128)(2,1)}, bf16[3,256,128]{2,1,0:T(8,128)(2,1)S(1)}, u32[]{:S(2)}, u32[]{:S(2)}) collective-permute-start(bf16[3,256,128]{2,1,0:T(8,128)(2,1)} %get-tuple-element.68), channel_id=1, source_target_pairs={{0,1},{1,2},{2,3},{3,4},{4,5},{5,6},{6,7},{7,0},{8,9},{9,10},{10,1... | collective-permute-start | bytes 589832 | tf_op jit(solution)/shard_map/ppermute | solution.py:239
  55.2 21.2 %collective-permute-start.1 = (bf16[3,256,128]{2,1,0:T(8,128)(2,1)}, bf16[3,256,128]{2,1,0:T(8,128)(2,1)S(1)}, u32[]{:S(2)}, u32[]{:S(2)}) collective-permute-start(bf16[3,256,128]{2,1,0:T(8,128)(2,1)} %get-tuple-element.69), channel_id=1, source_target_pairs={{0,2},{1,3},{2,4},{3,5},{4,6},{5,7},{6,0},{7,1},{8,10},{9,11},{10,... | collective-permute-start | bytes 589832 | tf_op jit(solution)/shard_map/ppermute | solution.py:239
  58.5 31.2 %collective-permute-start.2 = (bf16[3,256,128]{2,1,0:T(8,128)(2,1)}, bf16[3,256,128]{2,1,0:T(8,128)(2,1)S(1)}, u32[]{:S(2)}, u32[]{:S(2)}) collective-permute-start(bf16[3,256,128]{2,1,0:T(8,128)(2,1)} %get-tuple-element.70), channel_id=1, source_target_pairs={{0,3},{1,4},{2,5},{3,6},{4,7},{5,0},{6,1},{7,2},{8,11},{9,12},{10,... | collective-permute-start | bytes 589832 | tf_op jit(solution)/shard_map/ppermute | solution.py:239
  62.5 27.2 %collective-permute-start.3 = (bf16[3,256,128]{2,1,0:T(8,128)(2,1)}, bf16[3,256,128]{2,1,0:T(8,128)(2,1)S(1)}, u32[]{:S(2)}, u32[]{:S(2)}) collective-permute-start(bf16[3,256,128]{2,1,0:T(8,128)(2,1)} %get-tuple-element.71), channel_id=1, source_target_pairs={{0,4},{1,5},{2,6},{3,7},{4,0},{5,1},{6,2},{7,3},{8,12},{9,13},{10,... | collective-permute-start | bytes 589832 | tf_op jit(solution)/shard_map/ppermute | solution.py:239
  63.1 27.8 %collective-permute-start.4 = (bf16[3,256,128]{2,1,0:T(8,128)(2,1)}, bf16[3,256,128]{2,1,0:T(8,128)(2,1)S(1)}, u32[]{:S(2)}, u32[]{:S(2)}) collective-permute-start(bf16[3,256,128]{2,1,0:T(8,128)(2,1)} %get-tuple-element.72), channel_id=1, source_target_pairs={{0,5},{1,6},{2,7},{3,0},{4,1},{5,2},{6,3},{7,4},{8,13},{9,14},{10,... | collective-permute-start | bytes 589832 | tf_op jit(solution)/shard_map/ppermute | solution.py:239
  68.0 28.5 %collective-permute-start.5 = (bf16[3,256,128]{2,1,0:T(8,128)(2,1)}, bf16[3,256,128]{2,1,0:T(8,128)(2,1)S(1)}, u32[]{:S(2)}, u32[]{:S(2)}) collective-permute-start(bf16[3,256,128]{2,1,0:T(8,128)(2,1)} %get-tuple-element.73), channel_id=1, source_target_pairs={{0,6},{1,7},{2,0},{3,1},{4,2},{5,3},{6,4},{7,5},{8,14},{9,15},{10,... | collective-permute-start | bytes 589832 | tf_op jit(solution)/shard_map/ppermute | solution.py:239
  76.4 22.2 %collective-permute-start.6 = (bf16[3,256,128]{2,1,0:T(8,128)(2,1)}, bf16[3,256,128]{2,1,0:T(8,128)(2,1)S(1)}, u32[]{:S(2)}, u32[]{:S(2)}) collective-permute-start(bf16[3,256,128]{2,1,0:T(8,128)(2,1)} %get-tuple-element.74), channel_id=1, source_target_pairs={{0,7},{1,0},{2,1},{3,2},{4,3},{5,4},{6,5},{7,6},{8,15},{9,8},{10,9... | collective-permute-start | bytes 589832 | tf_op jit(solution)/shard_map/ppermute | solution.py:239
  148.8 152.0 %all-to-all-start.2 = ((bf16[32,3,128,128]{3,2,1,0:T(8,128)(2,1)}), bf16[32,3,128,128]{3,2,1,0:T(8,128)(2,1)S(1)}, u32[]{:S(2)}, u32[]{:S(2)}) async-start(bf16[32,3,128,128]{3,2,1,0:T(8,128)(2,1)} %shard_map.94.rest_0_), calls=%async_computation.2 | async-start | bytes 6291456 | tf_op jit(solution)/shard_map/all_to_all | solution.py:266
  206.0 11.6 %collective-permute-start.7 = (bf16[3,256,128]{2,1,0:T(8,128)(2,1)}, bf16[3,256,128]{2,1,0:T(8,128)(2,1)S(1)}, u32[]{:S(2)}, u32[]{:S(2)}) collective-permute-start(bf16[3,256,128]{2,1,0:T(8,128)(2,1)} %get-tuple-element.76), channel_id=1, source_target_pairs={{0,1},{1,2},{2,3},{3,4},{4,5},{5,6},{6,7},{7,0},{8,9},{9,10},{10,1... | collective-permute-start | bytes 589832 | tf_op jit(solution)/shard_map/ppermute | solution.py:239
  209.7 20.5 %collective-permute-start.8 = (bf16[3,256,128]{2,1,0:T(8,128)(2,1)}, bf16[3,256,128]{2,1,0:T(8,128)(2,1)S(1)}, u32[]{:S(2)}, u32[]{:S(2)}) collective-permute-start(bf16[3,256,128]{2,1,0:T(8,128)(2,1)} %get-tuple-element.77), channel_id=1, source_target_pairs={{0,2},{1,3},{2,4},{3,5},{4,6},{5,7},{6,0},{7,1},{8,10},{9,11},{10,... | collective-permute-start | bytes 589832 | tf_op jit(solution)/shard_map/ppermute | solution.py:239
  210.8 26.6 %collective-permute-start.9 = (bf16[3,256,128]{2,1,0:T(8,128)(2,1)}, bf16[3,256,128]{2,1,0:T(8,128)(2,1)}, u32[]{:S(2)}, u32[]{:S(2)}) collective-permute-start(bf16[3,256,128]{2,1,0:T(8,128)(2,1)} %get-tuple-element.78), channel_id=1, source_target_pairs={{0,3},{1,4},{2,5},{3,6},{4,7},{5,0},{6,1},{7,2},{8,11},{9,12},{10,... | collective-permute-start | bytes 589832 | tf_op jit(solution)/shard_map/ppermute | solution.py:239
  211.4 32.2 %collective-permute-start.10 = (bf16[3,256,128]{2,1,0:T(8,128)(2,1)}, bf16[3,256,128]{2,1,0:T(8,128)(2,1)}, u32[]{:S(2)}, u32[]{:S(2)}) collective-permute-start(bf16[3,256,128]{2,1,0:T(8,128)(2,1)} %get-tuple-element.79), channel_id=1, source_target_pairs={{0,4},{1,5},{2,6},{3,7},{4,0},{5,1},{6,2},{7,3},{8,12},{9,13},{10,... | collective-permute-start | bytes 589832 | tf_op jit(solution)/shard_map/ppermute | solution.py:239
  216.2 27.4 %collective-permute-start.11 = (bf16[3,256,128]{2,1,0:T(8,128)(2,1)}, bf16[3,256,128]{2,1,0:T(8,128)(2,1)}, u32[]{:S(2)}, u32[]{:S(2)}) collective-permute-start(bf16[3,256,128]{2,1,0:T(8,128)(2,1)} %get-tuple-element.80), channel_id=1, source_target_pairs={{0,5},{1,6},{2,7},{3,0},{4,1},{5,2},{6,3},{7,4},{8,13},{9,14},{10,... | collective-permute-start | bytes 589832 | tf_op jit(solution)/shard_map/ppermute | solution.py:239
  217.6 29.4 %collective-permute-start.12 = (bf16[3,256,128]{2,1,0:T(8,128)(2,1)}, bf16[3,256,128]{2,1,0:T(8,128)(2,1)}, u32[]{:S(2)}, u32[]{:S(2)}) collective-permute-start(bf16[3,256,128]{2,1,0:T(8,128)(2,1)} %get-tuple-element.81), channel_id=1, source_target_pairs={{0,6},{1,7},{2,0},{3,1},{4,2},{5,3},{6,4},{7,5},{8,14},{9,15},{10,... | collective-permute-start | bytes 589832 | tf_op jit(solution)/shard_map/ppermute | solution.py:239
  230.2 21.0 %collective-permute-start.13 = (bf16[3,256,128]{2,1,0:T(8,128)(2,1)}, bf16[3,256,128]{2,1,0:T(8,128)(2,1)}, u32[]{:S(2)}, u32[]{:S(2)}) collective-permute-start(bf16[3,256,128]{2,1,0:T(8,128)(2,1)} %get-tuple-element.82), channel_id=1, source_target_pairs={{0,7},{1,0},{2,1},{3,2},{4,3},{5,4},{6,5},{7,6},{8,15},{9,8},{10,9... | collective-permute-start | bytes 589832 | tf_op jit(solution)/shard_map/ppermute | solution.py:239
  300.8 150.0 %all-to-all-start.1 = ((bf16[32,3,128,128]{3,2,1,0:T(8,128)(2,1)}), bf16[32,3,128,128]{3,2,1,0:T(8,128)(2,1)}, u32[]{:S(2)}, u32[]{:S(2)}) async-start(bf16[32,3,128,128]{3,2,1,0:T(8,128)(2,1)} %shard_map.96.rest_0_), calls=%async_computation.1 | async-start | bytes 6291456 | tf_op jit(solution)/shard_map/all_to_all | solution.py:266
  358.3 11.6 %collective-permute-start.14 = (bf16[3,256,128]{2,1,0:T(8,128)(2,1)}, bf16[3,256,128]{2,1,0:T(8,128)(2,1)S(1)}, u32[]{:S(2)}, u32[]{:S(2)}) collective-permute-start(bf16[3,256,128]{2,1,0:T(8,128)(2,1)} %get-tuple-element.84), channel_id=1, source_target_pairs={{0,1},{1,2},{2,3},{3,4},{4,5},{5,6},{6,7},{7,0},{8,9},{9,10},{10,1... | collective-permute-start | bytes 589832 | tf_op jit(solution)/shard_map/ppermute | solution.py:239
  358.9 19.0 %collective-permute-start.15 = (bf16[3,256,128]{2,1,0:T(8,128)(2,1)}, bf16[3,256,128]{2,1,0:T(8,128)(2,1)S(1)}, u32[]{:S(2)}, u32[]{:S(2)}) collective-permute-start(bf16[3,256,128]{2,1,0:T(8,128)(2,1)} %get-tuple-element.85), channel_id=1, source_target_pairs={{0,2},{1,3},{2,4},{3,5},{4,6},{5,7},{6,0},{7,1},{8,10},{9,11},{10,... | collective-permute-start | bytes 589832 | tf_op jit(solution)/shard_map/ppermute | solution.py:239
  360.7 28.1 %collective-permute-start.16 = (bf16[3,256,128]{2,1,0:T(8,128)(2,1)}, bf16[3,256,128]{2,1,0:T(8,128)(2,1)}, u32[]{:S(2)}, u32[]{:S(2)}) collective-permute-start(bf16[3,256,128]{2,1,0:T(8,128)(2,1)} %get-tuple-element.86), channel_id=1, source_target_pairs={{0,3},{1,4},{2,5},{3,6},{4,7},{5,0},{6,1},{7,2},{8,11},{9,12},{10,... | collective-permute-start | bytes 589832 | tf_op jit(solution)/shard_map/ppermute | solution.py:239
  364.3 32.8 %collective-permute-start.17 = (bf16[3,256,128]{2,1,0:T(8,128)(2,1)}, bf16[3,256,128]{2,1,0:T(8,128)(2,1)}, u32[]{:S(2)}, u32[]{:S(2)}) collective-permute-start(bf16[3,256,128]{2,1,0:T(8,128)(2,1)} %get-tuple-element.87), channel_id=1, source_target_pairs={{0,4},{1,5},{2,6},{3,7},{4,0},{5,1},{6,2},{7,3},{8,12},{9,13},{10,... | collective-permute-start | bytes 589832 | tf_op jit(solution)/shard_map/ppermute | solution.py:239
  365.5 31.7 %collective-permute-start.18 = (bf16[3,256,128]{2,1,0:T(8,128)(2,1)}, bf16[3,256,128]{2,1,0:T(8,128)(2,1)}, u32[]{:S(2)}, u32[]{:S(2)}) collective-permute-start(bf16[3,256,128]{2,1,0:T(8,128)(2,1)} %get-tuple-element.88), channel_id=1, source_target_pairs={{0,5},{1,6},{2,7},{3,0},{4,1},{5,2},{6,3},{7,4},{8,13},{9,14},{10,... | collective-permute-start | bytes 589832 | tf_op jit(solution)/shard_map/ppermute | solution.py:239
  369.9 29.5 %collective-permute-start.19 = (bf16[3,256,128]{2,1,0:T(8,128)(2,1)}, bf16[3,256,128]{2,1,0:T(8,128)(2,1)}, u32[]{:S(2)}, u32[]{:S(2)}) collective-permute-start(bf16[3,256,128]{2,1,0:T(8,128)(2,1)} %get-tuple-element.89), channel_id=1, source_target_pairs={{0,6},{1,7},{2,0},{3,1},{4,2},{5,3},{6,4},{7,5},{8,14},{9,15},{10,... | collective-permute-start | bytes 589832 | tf_op jit(solution)/shard_map/ppermute | solution.py:239
  377.9 23.2 %collective-permute-start.20 = (bf16[3,256,128]{2,1,0:T(8,128)(2,1)}, bf16[3,256,128]{2,1,0:T(8,128)(2,1)}, u32[]{:S(2)}, u32[]{:S(2)}) collective-permute-start(bf16[3,256,128]{2,1,0:T(8,128)(2,1)} %get-tuple-element.90), channel_id=1, source_target_pairs={{0,7},{1,0},{2,1},{3,2},{4,3},{5,4},{6,5},{7,6},{8,15},{9,8},{10,9... | collective-permute-start | bytes 589832 | tf_op jit(solution)/shard_map/ppermute | solution.py:239
  450.8 45.5 %all-to-all-start = ((bf16[32,3,128,128]{3,2,1,0:T(8,128)(2,1)}), bf16[32,3,128,128]{3,2,1,0:T(8,128)(2,1)}, u32[]{:S(2)}, u32[]{:S(2)}) async-start(bf16[32,3,128,128]{3,2,1,0:T(8,128)(2,1)} %shard_map.98), calls=%async_computation | async-start | bytes 6291456 | tf_op jit(solution)/shard_map/all_to_all | solution.py:266
  496.3 47.2 %all-to-all-start.5 = ((bf16[32,3,128,128]{3,2,1,0:T(8,128)(2,1)}), bf16[32,3,128,128]{3,2,1,0:T(8,128)(2,1)}, u32[]{:S(2)}, u32[]{:S(2)}) async-start(bf16[32,3,128,128]{3,2,1,0:T(8,128)(2,1)} %copy-done), calls=%async_computation.5 | async-start | bytes 6291456 | tf_op jit(solution)/shard_map/all_to_all | solution.py:272
  543.5 46.3 %all-to-all-start.4 = ((bf16[32,3,128,128]{3,2,1,0:T(8,128)(2,1)}), bf16[32,3,128,128]{3,2,1,0:T(8,128)(2,1)}, u32[]{:S(2)}, u32[]{:S(2)}) async-start(bf16[32,3,128,128]{3,2,1,0:T(8,128)(2,1)} %get-tuple-element.103), calls=%async_computation.4 | async-start | bytes 6291456 | tf_op jit(solution)/shard_map/all_to_all | solution.py:272
  589.8 129.9 %all-to-all-start.3 = ((bf16[32,3,128,128]{3,2,1,0:T(8,128)(2,1)}), bf16[32,3,128,128]{3,2,1,0:T(8,128)(2,1)S(1)}, u32[]{:S(2)}, u32[]{:S(2)}) async-start(bf16[32,3,128,128]{3,2,1,0:T(8,128)(2,1)} %get-tuple-element.94), calls=%async_computation.3 | async-start | bytes 6291456 | tf_op jit(solution)/shard_map/all_to_all | solution.py:272
  647.2 11.6 %collective-permute-start.35 = (bf16[3,256,128]{2,1,0:T(8,128)(2,1)}, bf16[3,256,128]{2,1,0:T(8,128)(2,1)}, u32[]{:S(2)}, u32[]{:S(2)}) collective-permute-start(bf16[3,256,128]{2,1,0:T(8,128)(2,1)} %get-tuple-element.114), channel_id=1, source_target_pairs={{0,1},{1,2},{2,3},{3,4},{4,5},{5,6},{6,7},{7,0},{8,9},{9,10},{10,1... | collective-permute-start | bytes 589832 | tf_op jit(solution)/shard_map/ppermute | solution.py:239
  650.7 60.0 %collective-permute-start.36 = (bf16[3,256,128]{2,1,0:T(8,128)(2,1)}, bf16[3,256,128]{2,1,0:T(8,128)(2,1)S(1)}, u32[]{:S(2)}, u32[]{:S(2)}) collective-permute-start(bf16[3,256,128]{2,1,0:T(8,128)(2,1)} %get-tuple-element.115), channel_id=1, source_target_pairs={{0,2},{1,3},{2,4},{3,5},{4,6},{5,7},{6,0},{7,1},{8,10},{9,11},{10,... | collective-permute-start | bytes 589832 | tf_op jit(solution)/shard_map/ppermute | solution.py:239
  651.9 60.6 %collective-permute-start.37 = (bf16[3,256,128]{2,1,0:T(8,128)(2,1)}, bf16[3,256,128]{2,1,0:T(8,128)(2,1)S(1)}, u32[]{:S(2)}, u32[]{:S(2)}) collective-permute-start(bf16[3,256,128]{2,1,0:T(8,128)(2,1)} %get-tuple-element.116), channel_id=1, source_target_pairs={{0,3},{1,4},{2,5},{3,6},{4,7},{5,0},{6,1},{7,2},{8,11},{9,12},{10,... | collective-permute-start | bytes 589832 | tf_op jit(solution)/shard_map/ppermute | solution.py:239
  652.5 60.7 %collective-permute-start.38 = (bf16[3,256,128]{2,1,0:T(8,128)(2,1)}, bf16[3,256,128]{2,1,0:T(8,128)(2,1)}, u32[]{:S(2)}, u32[]{:S(2)}) collective-permute-start(bf16[3,256,128]{2,1,0:T(8,128)(2,1)} %get-tuple-element.117), channel_id=1, source_target_pairs={{0,4},{1,5},{2,6},{3,7},{4,0},{5,1},{6,2},{7,3},{8,12},{9,13},{10,... | collective-permute-start | bytes 589832 | tf_op jit(solution)/shard_map/ppermute | solution.py:239
  657.2 57.1 %collective-permute-start.39 = (bf16[3,256,128]{2,1,0:T(8,128)(2,1)}, bf16[3,256,128]{2,1,0:T(8,128)(2,1)}, u32[]{:S(2)}, u32[]{:S(2)}) collective-permute-start(bf16[3,256,128]{2,1,0:T(8,128)(2,1)} %get-tuple-element.118), channel_id=1, source_target_pairs={{0,5},{1,6},{2,7},{3,0},{4,1},{5,2},{6,3},{7,4},{8,13},{9,14},{10,... | collective-permute-start | bytes 589832 | tf_op jit(solution)/shard_map/ppermute | solution.py:239
  658.8 59.7 %collective-permute-start.40 = (bf16[3,256,128]{2,1,0:T(8,128)(2,1)}, bf16[3,256,128]{2,1,0:T(8,128)(2,1)}, u32[]{:S(2)}, u32[]{:S(2)}) collective-permute-start(bf16[3,256,128]{2,1,0:T(8,128)(2,1)} %get-tuple-element.119), channel_id=1, source_target_pairs={{0,6},{1,7},{2,0},{3,1},{4,2},{5,3},{6,4},{7,5},{8,14},{9,15},{10,... | collective-permute-start | bytes 589832 | tf_op jit(solution)/shard_map/ppermute | solution.py:239
  710.7 60.2 %collective-permute-start.41 = (bf16[3,256,128]{2,1,0:T(8,128)(2,1)}, bf16[3,256,128]{2,1,0:T(8,128)(2,1)}, u32[]{:S(2)}, u32[]{:S(2)}) collective-permute-start(bf16[3,256,128]{2,1,0:T(8,128)(2,1)} %get-tuple-element.120), channel_id=1, source_target_pairs={{0,7},{1,0},{2,1},{3,2},{4,3},{5,4},{6,5},{7,6},{8,15},{9,8},{10,9... | collective-permute-start | bytes 589832 | tf_op jit(solution)/shard_map/ppermute | solution.py:239
  712.5 61.9 %collective-permute-start.28 = (bf16[3,256,128]{2,1,0:T(8,128)(2,1)}, bf16[3,256,128]{2,1,0:T(8,128)(2,1)S(1)}, u32[]{:S(2)}, u32[]{:S(2)}) collective-permute-start(bf16[3,256,128]{2,1,0:T(8,128)(2,1)} %get-tuple-element.105), channel_id=1, source_target_pairs={{0,1},{1,2},{2,3},{3,4},{4,5},{5,6},{6,7},{7,0},{8,9},{9,10},{10,1... | collective-permute-start | bytes 589832 | tf_op jit(solution)/shard_map/ppermute | solution.py:239
  713.2 65.2 %collective-permute-start.29 = (bf16[3,256,128]{2,1,0:T(8,128)(2,1)}, bf16[3,256,128]{2,1,0:T(8,128)(2,1)S(1)}, u32[]{:S(2)}, u32[]{:S(2)}) collective-permute-start(bf16[3,256,128]{2,1,0:T(8,128)(2,1)} %get-tuple-element.106), channel_id=1, source_target_pairs={{0,2},{1,3},{2,4},{3,5},{4,6},{5,7},{6,0},{7,1},{8,10},{9,11},{10,... | collective-permute-start | bytes 589832 | tf_op jit(solution)/shard_map/ppermute | solution.py:239
  714.3 64.3 %collective-permute-start.30 = (bf16[3,256,128]{2,1,0:T(8,128)(2,1)}, bf16[3,256,128]{2,1,0:T(8,128)(2,1)}, u32[]{:S(2)}, u32[]{:S(2)}) collective-permute-start(bf16[3,256,128]{2,1,0:T(8,128)(2,1)} %get-tuple-element.107), channel_id=1, source_target_pairs={{0,3},{1,4},{2,5},{3,6},{4,7},{5,0},{6,1},{7,2},{8,11},{9,12},{10,... | collective-permute-start | bytes 589832 | tf_op jit(solution)/shard_map/ppermute | solution.py:239
  718.4 61.9 %collective-permute-start.31 = (bf16[3,256,128]{2,1,0:T(8,128)(2,1)}, bf16[3,256,128]{2,1,0:T(8,128)(2,1)}, u32[]{:S(2)}, u32[]{:S(2)}) collective-permute-start(bf16[3,256,128]{2,1,0:T(8,128)(2,1)} %get-tuple-element.108), channel_id=1, source_target_pairs={{0,4},{1,5},{2,6},{3,7},{4,0},{5,1},{6,2},{7,3},{8,12},{9,13},{10,... | collective-permute-start | bytes 589832 | tf_op jit(solution)/shard_map/ppermute | solution.py:239
  770.9 17.9 %collective-permute-start.32 = (bf16[3,256,128]{2,1,0:T(8,128)(2,1)}, bf16[3,256,128]{2,1,0:T(8,128)(2,1)S(1)}, u32[]{:S(2)}, u32[]{:S(2)}) collective-permute-start(bf16[3,256,128]{2,1,0:T(8,128)(2,1)} %get-tuple-element.109), channel_id=1, source_target_pairs={{0,5},{1,6},{2,7},{3,0},{4,1},{5,2},{6,3},{7,4},{8,13},{9,14},{10,... | collective-permute-start | bytes 589832 | tf_op jit(solution)/shard_map/ppermute | solution.py:239
  774.4 21.1 %collective-permute-start.33 = (bf16[3,256,128]{2,1,0:T(8,128)(2,1)}, bf16[3,256,128]{2,1,0:T(8,128)(2,1)S(1)}, u32[]{:S(2)}, u32[]{:S(2)}) collective-permute-start(bf16[3,256,128]{2,1,0:T(8,128)(2,1)} %get-tuple-element.110), channel_id=1, source_target_pairs={{0,6},{1,7},{2,0},{3,1},{4,2},{5,3},{6,4},{7,5},{8,14},{9,15},{10,... | collective-permute-start | bytes 589832 | tf_op jit(solution)/shard_map/ppermute | solution.py:239
  778.3 26.1 %collective-permute-start.34 = (bf16[3,256,128]{2,1,0:T(8,128)(2,1)}, bf16[3,256,128]{2,1,0:T(8,128)(2,1)S(1)}, u32[]{:S(2)}, u32[]{:S(2)}) collective-permute-start(bf16[3,256,128]{2,1,0:T(8,128)(2,1)} %get-tuple-element.111), channel_id=1, source_target_pairs={{0,7},{1,0},{2,1},{3,2},{4,3},{5,4},{6,5},{7,6},{8,15},{9,8},{10,9... | collective-permute-start | bytes 589832 | tf_op jit(solution)/shard_map/ppermute | solution.py:239
  778.6 27.6 %collective-permute-start.21 = (bf16[3,256,128]{2,1,0:T(8,128)(2,1)}, bf16[3,256,128]{2,1,0:T(8,128)(2,1)S(1)}, u32[]{:S(2)}, u32[]{:S(2)}) collective-permute-start(bf16[3,256,128]{2,1,0:T(8,128)(2,1)} %get-tuple-element.96), channel_id=1, source_target_pairs={{0,1},{1,2},{2,3},{3,4},{4,5},{5,6},{6,7},{7,0},{8,9},{9,10},{10,1... | collective-permute-start | bytes 589832 | tf_op jit(solution)/shard_map/ppermute | solution.py:239
  780.4 25.8 %collective-permute-start.22 = (bf16[3,256,128]{2,1,0:T(8,128)(2,1)}, bf16[3,256,128]{2,1,0:T(8,128)(2,1)S(1)}, u32[]{:S(2)}, u32[]{:S(2)}) collective-permute-start(bf16[3,256,128]{2,1,0:T(8,128)(2,1)} %get-tuple-element.97), channel_id=1, source_target_pairs={{0,2},{1,3},{2,4},{3,5},{4,6},{5,7},{6,0},{7,1},{8,10},{9,11},{10,... | collective-permute-start | bytes 589832 | tf_op jit(solution)/shard_map/ppermute | solution.py:239
  788.9 119.3 %collective-permute-start.23 = (bf16[3,256,128]{2,1,0:T(8,128)(2,1)}, bf16[3,256,128]{2,1,0:T(8,128)(2,1)S(1)}, u32[]{:S(2)}, u32[]{:S(2)}) collective-permute-start(bf16[3,256,128]{2,1,0:T(8,128)(2,1)} %get-tuple-element.98), channel_id=1, source_target_pairs={{0,3},{1,4},{2,5},{3,6},{4,7},{5,0},{6,1},{7,2},{8,11},{9,12},{10,... | collective-permute-start | bytes 589832 | tf_op jit(solution)/shard_map/ppermute | solution.py:239
  795.5 112.7 %collective-permute-start.24 = (bf16[3,256,128]{2,1,0:T(8,128)(2,1)}, bf16[3,256,128]{2,1,0:T(8,128)(2,1)S(1)}, u32[]{:S(2)}, u32[]{:S(2)}) collective-permute-start(bf16[3,256,128]{2,1,0:T(8,128)(2,1)} %get-tuple-element.99), channel_id=1, source_target_pairs={{0,4},{1,5},{2,6},{3,7},{4,0},{5,1},{6,2},{7,3},{8,12},{9,13},{10,... | collective-permute-start | bytes 589832 | tf_op jit(solution)/shard_map/ppermute | solution.py:239
  804.5 103.7 %collective-permute-start.25 = (bf16[3,256,128]{2,1,0:T(8,128)(2,1)}, bf16[3,256,128]{2,1,0:T(8,128)(2,1)S(1)}, u32[]{:S(2)}, u32[]{:S(2)}) collective-permute-start(bf16[3,256,128]{2,1,0:T(8,128)(2,1)} %get-tuple-element.100), channel_id=1, source_target_pairs={{0,5},{1,6},{2,7},{3,0},{4,1},{5,2},{6,3},{7,4},{8,13},{9,14},{10,... | collective-permute-start | bytes 589832 | tf_op jit(solution)/shard_map/ppermute | solution.py:239
  806.2 102.0 %collective-permute-start.26 = (bf16[3,256,128]{2,1,0:T(8,128)(2,1)}, bf16[3,256,128]{2,1,0:T(8,128)(2,1)S(1)}, u32[]{:S(2)}, u32[]{:S(2)}) collective-permute-start(bf16[3,256,128]{2,1,0:T(8,128)(2,1)} %get-tuple-element.101), channel_id=1, source_target_pairs={{0,6},{1,7},{2,0},{3,1},{4,2},{5,3},{6,4},{7,5},{8,14},{9,15},{10,... | collective-permute-start | bytes 589832 | tf_op jit(solution)/shard_map/ppermute | solution.py:239
  806.2 102.0 %collective-permute-start.27 = (bf16[3,256,128]{2,1,0:T(8,128)(2,1)}, bf16[3,256,128]{2,1,0:T(8,128)(2,1)S(1)}, u32[]{:S(2)}, u32[]{:S(2)}) collective-permute-start(bf16[3,256,128]{2,1,0:T(8,128)(2,1)} %get-tuple-element.102), channel_id=1, source_target_pairs={{0,7},{1,0},{2,1},{3,2},{4,3},{5,4},{6,5},{7,6},{8,15},{9,8},{10,9... | collective-permute-start | bytes 589832 | tf_op jit(solution)/shard_map/ppermute | solution.py:239
  (30 other events, 772.3 us)
